TPU v7x, 256 devices: a whole 4x4x8 slice. The times are simulated.
256 devices in a mesh: aux: 4 (over x), row: 16 (over z_hi, y), col: 4 (over z_lo, core).
Axes of the slice: x: 4, y: 4, z: 8 (z_hi: 4, z_lo: 2; z = z_hi * 2 + z_lo), core: 2. Of those that a mesh axis runs over, the one named last changes fastest.
Arguments:
- factors: bfloat16 [8, 4, 2560, 10240], P('aux', None, 'row', 'col'), may hold values from -0.078125 to 0.078125
- orbitals: bfloat16 [10240, 512], P('col'), may hold values from -0.25 to 0.25
- tile_mask: int32 [8, 80, 80], P('aux'), may hold values from 0 to 1, as said below
Outputs:
- exchange: float32 [10240, 10240], P(('aux', 'row'), 'col')
Inputs may be any that keep to these rules, and one draw needn't show every extreme that they name: `tile_mask`: 0 or 1; present tiles cluster around a centre tile drawn for each auxiliary function, and absent tiles occur everywhere.
All inputs are finite; a program needn't handle non-finite values.
Results may differ from a plain program's by a relative error of at most 0.02.
Values may be sent and summed in bfloat16 or wider, within the bound.
A program may use at most 64 MiB of HBM per device.

v0:
```python
import jax
import jax.numpy as jnp
from jax import lax
from jax.sharding import PartitionSpec as P

NB = 10240
TILE = 128


def on_device(factors, orbitals, tile_mask):
    local_count = factors.shape[0]
    aux_parts = factors.shape[1]
    row_len = factors.shape[2]
    col_len = factors.shape[3]
    occ_count = orbitals.shape[1]
    row_index = lax.axis_index("row")
    col_index = lax.axis_index("col")
    tile_cols = col_len // TILE
    basis_rows = (
        jnp.arange(aux_parts, dtype=jnp.int32)[:, None] * (NB // aux_parts)
        + row_index * row_len
        + jnp.arange(row_len, dtype=jnp.int32)[None, :]
    ) // TILE
    row_tiles = jnp.take(tile_mask, basis_rows, axis=1)
    local_tiles = lax.dynamic_slice_in_dim(row_tiles, col_index * tile_cols, tile_cols, axis=3)
    masked = (
        factors.reshape(local_count, aux_parts, row_len, tile_cols, TILE)
        * local_tiles.astype(jnp.bfloat16)[..., None]
    )
    masked = masked.reshape(factors.shape)
    partial_orb = jnp.einsum("qatn,nk->atqk", masked, orbitals, preferred_element_type=jnp.float32)
    own_panel = lax.psum_scatter(
        partial_orb.astype(jnp.bfloat16), "col", scatter_dimension=0, tiled=True
    )
    row_panel = lax.all_gather(own_panel, "col", axis=0, tiled=True)
    rows_three = row_panel.reshape(aux_parts * row_len, local_count, occ_count)
    cols_three = own_panel.reshape(row_len, local_count, occ_count)
    zeros_k = jnp.zeros((aux_parts * row_len, col_len), jnp.float32)

    def one_function(function_index, summed):
        left_rows = lax.dynamic_index_in_dim(rows_three, function_index, 1, keepdims=False)
        right_rows = lax.dynamic_index_in_dim(cols_three, function_index, 1, keepdims=False)
        return summed + lax.dot_general(
            left_rows,
            lax.all_gather(right_rows, "row", axis=0, tiled=True),
            (((1,), (1,)), ((), ())),
            preferred_element_type=jnp.float32,
        )

    partial_k = lax.fori_loop(0, local_count, one_function, zeros_k)
    return lax.psum_scatter(
        partial_k.astype(jnp.bfloat16), "aux", scatter_dimension=0, tiled=True
    ).astype(jnp.float32)


def solution(mesh):
    placed = (P("aux", None, "row", "col"), P("col", None), P("aux", None, None))
    return jax.shard_map(
        on_device, mesh=mesh, in_specs=placed, out_specs=P(("aux", "row"), "col"), check_vma=False
    )
```

profile of v0, /device:TPU:1, one launch (start us, length us, event | category | flops | bytes accessed | tf_op | source)
XLA Modules:
  0.0 320.6 jit_solution(14469421907034454084)
XLA Ops:
  6.5 0.0 copy-start
  6.5 0.0 all-reduce.3.cloned.1.call-start
  6.5 0.1 compare_select_fusion
  6.6 0.1 compare_and_fusion
  6.7 0.1 reshape.123
  6.8 3.4 %gather_fusion = s32[640,2,80]{2,0,1:T(8,128)S(1)} fusion(s32[2,80,80]{2,1,0:T(8,128)} %param.7, s32[1024]{0:T(1024)S(1)} %pad_clamp_fusion), kind=kCustom, calls=%fused_computation | custom fusion | bytes 821760 | tf_op jit(solution)/shard_map/jit(_take)/gather | solution.py:24
  10.2 0.3 fusion.18
  10.5 6.8 %mul.28 = bf16[2,4,160,20,128]{4,3,2,1,0:T(8,128)(2,1)} broadcast(bf16[2,4,160,20]{3,2,1,0:T(8,128)(2,1)S(1)} %fusion.18), dimensions={0,1,2,3} | broadcast | bytes 6604800 | tf_op jit(solution)/shard_map/mul | solution.py:27
  17.3 12.0 %mul.29 = bf16[2,4,160,2560]{3,2,1,0:T(8,128)(2,1)} reshape(bf16[2,4,160,20,128]{4,3,2,1,0:T(8,128)(2,1)} %mul.28) | data formatting | bytes 13107200 | tf_op jit(solution)/shard_map/mul | solution.py:27
  29.3 0.0 copy-done
  29.3 0.0 copy-start.1
  29.3 9.4 %fusion.12 = bf16[4,160,2,512]{3,1,0,2:T(8,128)(2,1)} fusion(bf16[2560,512]{1,0:T(8,128)(2,1)S(1)} %copy-done, bf16[2,4,160,2560]{3,2,1,0:T(8,128)(2,1)} %param.5, bf16[2,4,160,2560]{3,2,1,0:T(8,128)(2,1)} %mul.29), kind=kOutput, calls=%fused_computation.11 | convolution fusion | flops 3359375360 | bytes 17039360 | tf_op jit(solution)/shard_map/qatn,nk->atqk/dot_general | solution.py:31
  38.6 0.0 all-reduce.3.cloned.1.call-update
  38.7 0.0 all-gather.7.cloned.1.call-start
  38.7 0.0 copy-done.1
  38.7 0.6 dynamic-slice.1
  39.3 53.3 %all-reduce.3.cloned.1.call-done = bf16[4,160,2,512]{3,1,0,2:T(8,128)(2,1)} async-done(((bf16[4,160,2,512]{3,1,0,2:T(8,128)(2,1)}), bf16[4,160,2,512]{3,1,0,2:T(8,128)(2,1)}) %all-reduce.3.cloned.1.call-update) | async-done | bytes 1310736
  92.6 2.4 constant_dynamic-slice_fusion.1
  95.0 0.0 all-gather.7.cloned.1.call-update
  95.0 1.6 fusion.25
  96.6 24.2 %all-gather.7.cloned.1.call-done = bf16[4,160,2,512]{3,1,0,2:T(8,128)(2,1)} async-done(((bf16[1,160,2,512]{3,1,0,2:T(8,128)(2,1)}), bf16[4,160,2,512]{3,1,0,2:T(8,128)(2,1)}) %all-gather.7.cloned.1.call-update) | async-done | bytes 1310736 | tf_op jit(solution)/shard_map/all_gather | solution.py:35
  120.9 145.5 %while.14 = (s32[]{:T(128)}, f32[640,2560]{1,0:T(8,128)}, bf16[640,2,512]{2,0,1:T(8,128)(2,1)}, bf16[160,2,512]{2,0,1:T(8,128)(2,1)S(1)}, s32[]{:T(128)}, /*index=5*/s32[]{:T(128)}) while((s32[]{:T(128)}, f32[640,2560]{1,0:T(8,128)}, bf16[640,2,512]{2,0,1:T(8,128)(2,1)}, bf16[160,2,512]{2,0,1:T(8,128)(2,1)S(1)}, s32[]{:T(128)}, ...), condition=%wide.region_2.3_spmd.clone, body=%wide.region_1.2_spmd.clone.sunk | while | flops 1680998400 | bytes 25067656 | solution.py:50
  120.9 0.0 all-gather.9.cloned.1.call-start
  120.9 0.7 constant_dynamic-slice_fusion.3
  121.6 0.0 all-gather.9.cloned.1.call-update
  121.6 65.5 %all-gather.9.cloned.1.call-done = bf16[2560,1,512]{2,0,1:T(8,128)(2,1)} async-done(((bf16[160,1,512]{2,0,1:T(8,128)(2,1)}), bf16[2560,1,512]{2,0,1:T(8,128)(2,1)}) %all-gather.9.cloned.1.call-update) | async-done | bytes 2621456 | tf_op jit(solution)/shard_map/while/body/eval_jaxpr/all_gather | solution.py:45
  187.1 6.6 %select_add_fusion.2 = f32[640,2560]{1,0:T(8,128)} fusion(f32[640,2560]{1,0:T(8,128)} %get-tuple-element.144, pred[]{:T(512)S(6)} %compare.17, bf16[2560,1,512]{2,0,1:T(8,128)(2,1)} %all-gather.9.cloned.1.call-done, bf16[640,2,512]{2,0,1:T(8,128)(2,1)} %get-tuple-element.151, s32[]{:T(128)S(6)} %copy.12), kind=kOutput, calls=%fused_computation.1.clone.1 | convolution fusion | flops 1680998400 | bytes 16384005 | tf_op jit(solution)/shard_map/while/body/eval_jaxpr/dot_general | solution.py:43
  193.7 0.0 all-gather.9.cloned.1.call-start
  193.7 0.7 constant_dynamic-slice_fusion.3
  194.4 0.0 all-gather.9.cloned.1.call-update
  194.4 63.4 %all-gather.9.cloned.1.call-done = bf16[2560,1,512]{2,0,1:T(8,128)(2,1)} async-done(((bf16[160,1,512]{2,0,1:T(8,128)(2,1)}), bf16[2560,1,512]{2,0,1:T(8,128)(2,1)}) %all-gather.9.cloned.1.call-update) | async-done | bytes 2621456 | tf_op jit(solution)/shard_map/while/body/eval_jaxpr/all_gather | solution.py:45
  257.9 8.5 %select_add_fusion.2 = f32[640,2560]{1,0:T(8,128)} fusion(f32[640,2560]{1,0:T(8,128)} %get-tuple-element.144, pred[]{:T(512)S(6)} %compare.17, bf16[2560,1,512]{2,0,1:T(8,128)(2,1)} %all-gather.9.cloned.1.call-done, bf16[640,2,512]{2,0,1:T(8,128)(2,1)} %get-tuple-element.151, s32[]{:T(128)S(6)} %copy.12), kind=kOutput, calls=%fused_computation.1.clone.1 | convolution fusion | flops 1680998400 | bytes 16384005 | tf_op jit(solution)/shard_map/while/body/eval_jaxpr/dot_general | solution.py:43
  266.4 0.0 reduce-scatter.5.cloned.1.call-start
  266.4 5.0 %convert_element_type.18 = bf16[640,2560]{1,0:T(8,128)(2,1)} convert(f32[640,2560]{1,0:T(8,128)} %get-tuple-element.84) | non-fusion elementwise | flops 1638400 | bytes 9830400 | tf_op jit(solution)/shard_map/convert_element_type | solution.py:52
  271.4 0.0 reduce-scatter.5.cloned.1.call-update
  271.4 40.2 %reduce-scatter.5.cloned.1.call-done = bf16[160,2560]{1,0:T(8,128)(2,1)} async-done(((bf16[640,2560]{1,0:T(8,128)(2,1)}), bf16[160,2560]{1,0:T(8,128)(2,1)}) %reduce-scatter.5.cloned.1.call-update) | async-done | bytes 819216 | tf_op jit(solution)/shard_map/reduce_scatter | solution.py:51
  311.6 2.5 convert_element_type.19
  (3 shorter events, 0.0 us)
Async XLA Ops:
  6.5 22.7 %copy-start = (bf16[2560,512]{1,0:T(8,128)(2,1)S(1)}, bf16[2560,512]{1,0:T(8,128)(2,1)}, u32[]{:S(2)}) copy-start(bf16[2560,512]{1,0:T(8,128)(2,1)} %param.6) | copy-start | bytes 7864324
  6.5 86.1 %all-reduce.3.cloned.1.call-start = ((), (), s32[]{:S(2)}) async-start(), calls=%async_computation.3 | async-start | bytes 2621440
  29.3 9.4 %copy-start.1 = (u32[256]{0:T(256)S(1)}, u32[256]{0:T(256)}, u32[]{:S(2)}) copy-start(u32[256]{0:T(256)} %constant.82) | copy-start | bytes 3076
  38.7 82.2 %all-gather.7.cloned.1.call-start = ((), (), s32[]{:S(2)}) async-start(), calls=%async_computation.1 | async-start | bytes 1638400 | tf_op jit(solution)/shard_map/all_gather | solution.py:35
  120.9 66.3 %all-gather.9.cloned.1.call-start = ((), (), s32[]{:S(2)}) async-start(), calls=%async_computation.4 | async-start | bytes 2785280 | tf_op jit(solution)/shard_map/while/body/eval_jaxpr/all_gather | solution.py:45
  193.7 64.2 %all-gather.9.cloned.1.call-start = ((), (), s32[]{:S(2)}) async-start(), calls=%async_computation.4 | async-start | bytes 2785280 | tf_op jit(solution)/shard_map/while/body/eval_jaxpr/all_gather | solution.py:45
  266.4 45.2 %reduce-scatter.5.cloned.1.call-start = ((), (), s32[]{:S(2)}) async-start(), calls=%async_computation.2 | async-start | bytes 4096000 | tf_op jit(solution)/shard_map/reduce_scatter | solution.py:51
Sparse Core Ops, SparseCore 0:
  38.8 53.7 all-reduce.2
  95.1 25.7 all-gather.6
  124.1 62.9 all-gather.8
  196.7 61.1 all-gather.8
  271.5 40.0 reduce-scatter.4
where the time goes:
time: 321 us
  waiting for transfers between devices  247 us (77%)
  local copies, waits for them, and re-layouts  28.2 us (9%)
  matrix products  24.4 us (8%)
  between operations  13.2 us (4%)
  other arithmetic  7.97 us (2%)
    all_gather x2, waiting for transfers between devices, one_function(): lax.all_gather(right_rows, 'row', axis=0, tiled=True)  129 us
    unnamed x4, waiting for transfers between devices  53.3 us
    reduce_scatter x1, waiting for transfers between devices, on_device(): lax.psum_scatter(partial_k.astype(jnp.bfloat16), 'aux', scatter_dimension...  40.2 us
    all_gather x1, waiting for transfers between devices, on_device(): row_panel = lax.all_gather(own_panel, 'col', axis=0, tiled=True)  24.2 us
    mul x2, local copies, waits for them, and re-layouts, on_device(): factors.reshape(local_count, aux_parts, row_len, tile_cols, TILE)  18.7 us
    dot_general x2, matrix products, one_function(): lax.dot_general(left_rows, lax.all_gather(right_rows, 'row', axis=0, tile...  15.1 us
    dot_general x1, matrix products, on_device(): jnp.einsum('qatn,nk->atqk', masked, orbitals, preferred_element_type=jnp....  9.36 us
  transfers between devices with their start and end apart: 5, of which 5 were waited for; matrix products, arithmetic and copies ran while one was open for 1% of the time, Pallas kernels for 0%

commit v1 on v0

--- a/solution.py
+++ b/solution.py
@@ -42,7 +42,9 @@
         right_rows = lax.dynamic_index_in_dim(cols_three, function_index, 1, keepdims=False)
         return summed + lax.dot_general(
             left_rows,
-            lax.all_gather(right_rows, "row", axis=0, tiled=True),
+            jnp.concatenate(
+                lax.all_to_all(jnp.stack([right_rows] * lax.axis_size("row")), "row", 0, 0), axis=0
+            ),
             (((1,), (1,)), ((), ())),
             preferred_element_type=jnp.float32,
         )

time: 321 us -> 332 us (1.034)
  starting transfers between devices: 0.05 us -> 21.5 us
  waiting for transfers between devices: 247 us -> 234 us
    all_gather x2 -> x0, waiting for transfers between devices: 129 us -> none  [one_function(): lax.all_gather(right_rows, 'row', axis=0, tiled=True)]
    all_to_all x0 -> x2, waiting for transfers between devices: none -> 97.6 us  [one_function(): lax.all_to_all(jnp.stack([right_rows] * lax.axis_size('row')), 'row', 0, 0)]
    all_to_all x0 -> x2, starting transfers between devices: none -> 21.4 us  [one_function(): lax.all_to_all(jnp.stack([right_rows] * lax.axis_size('row')), 'row', 0, 0)]
    reduce_scatter x1, waiting for transfers between devices: 40.2 us -> 59.2 us  [on_device(): lax.psum_scatter(partial_k.astype(jnp.bfloat16), 'aux', scatter_dimension...]
    another operation x0 -> x4, local copies, waits for them, and re-layouts: none -> 3.46 us  [one_function(): jnp.stack([right_rows] * lax.axis_size('row'))]
where the time goes in v1:
time: 332 us
  waiting for transfers between devices  234 us (70%)
  local copies, waits for them, and re-layouts  30.4 us (9%)
  matrix products  24.5 us (7%)
  starting transfers between devices  21.5 us (6%)
  between operations  13.2 us (4%)
  other arithmetic  7.95 us (2%)
    all_to_all x2, waiting for transfers between devices, one_function(): lax.all_to_all(jnp.stack([right_rows] * lax.axis_size('row')), 'row', 0, 0)  97.6 us
    reduce_scatter x1, waiting for transfers between devices, on_device(): lax.psum_scatter(partial_k.astype(jnp.bfloat16), 'aux', scatter_dimension...  59.2 us
    unnamed x4, waiting for transfers between devices  53.2 us
    all_gather x1, waiting for transfers between devices, on_device(): row_panel = lax.all_gather(own_panel, 'col', axis=0, tiled=True)  24.1 us
    all_to_all x2, starting transfers between devices, one_function(): lax.all_to_all(jnp.stack([right_rows] * lax.axis_size('row')), 'row', 0, 0)  21.4 us
    mul x2, local copies, waits for them, and re-layouts, on_device(): factors.reshape(local_count, aux_parts, row_len, tile_cols, TILE)  18.7 us
    dot_general x2, matrix products, one_function(): lax.dot_general(left_rows, jnp.concatenate(lax.all_to_all(jnp.stack([righ...  15.1 us
    dot_general x1, matrix products, on_device(): jnp.einsum('qatn,nk->atqk', masked, orbitals, preferred_element_type=jnp....  9.36 us
  transfers between devices with their start and end apart: 5, of which 5 were waited for; matrix products, arithmetic and copies ran while one was open for 1% of the time, Pallas kernels for 0%

profile of v1, /device:TPU:1, one launch (start us, length us, event | category | flops | bytes accessed | tf_op | source)
XLA Modules:
  0.0 331.8 jit_solution(14648665257185578240)
XLA Ops:
  6.5 0.0 copy-start
  6.5 0.0 all-reduce.3.cloned.1.call-start
  6.5 0.1 compare_select_fusion
  6.6 0.1 compare_and_fusion
  6.7 0.1 reshape.135
  6.8 3.4 %gather_fusion = s32[640,2,80]{2,0,1:T(8,128)S(1)} fusion(s32[2,80,80]{2,1,0:T(8,128)} %param.7, s32[1024]{0:T(1024)S(1)} %pad_clamp_fusion), kind=kCustom, calls=%fused_computation | custom fusion | bytes 821760 | tf_op jit(solution)/shard_map/jit(_take)/gather | solution.py:24
  10.2 0.3 fusion.17
  10.5 6.8 %mul.28 = bf16[2,4,160,20,128]{4,3,2,1,0:T(8,128)(2,1)} broadcast(bf16[2,4,160,20]{3,2,1,0:T(8,128)(2,1)S(1)} %fusion.17), dimensions={0,1,2,3} | broadcast | bytes 6604800 | tf_op jit(solution)/shard_map/mul | solution.py:27
  17.3 12.0 %mul.29 = bf16[2,4,160,2560]{3,2,1,0:T(8,128)(2,1)} reshape(bf16[2,4,160,20,128]{4,3,2,1,0:T(8,128)(2,1)} %mul.28) | data formatting | bytes 13107200 | tf_op jit(solution)/shard_map/mul | solution.py:27
  29.3 0.0 copy-done
  29.3 0.0 copy-start.1
  29.3 9.4 %fusion.11 = bf16[4,160,2,512]{3,1,0,2:T(8,128)(2,1)} fusion(bf16[2560,512]{1,0:T(8,128)(2,1)S(1)} %copy-done, bf16[2,4,160,2560]{3,2,1,0:T(8,128)(2,1)} %param.5, bf16[2,4,160,2560]{3,2,1,0:T(8,128)(2,1)} %mul.29), kind=kOutput, calls=%fused_computation.10 | convolution fusion | flops 3359375360 | bytes 17039360 | tf_op jit(solution)/shard_map/qatn,nk->atqk/dot_general | solution.py:31
  38.6 0.0 all-reduce.3.cloned.1.call-update
  38.7 0.0 all-gather.2.cloned.1.call-start
  38.7 0.0 copy-done.1
  38.7 0.7 dynamic-slice.1
  39.4 53.2 %all-reduce.3.cloned.1.call-done = bf16[4,160,2,512]{3,1,0,2:T(8,128)(2,1)} async-done(((bf16[4,160,2,512]{3,1,0,2:T(8,128)(2,1)}), bf16[4,160,2,512]{3,1,0,2:T(8,128)(2,1)}) %all-reduce.3.cloned.1.call-update) | async-done | bytes 1310736
  92.6 2.4 constant_dynamic-slice_fusion
  95.0 0.0 all-gather.2.cloned.1.call-update
  95.0 0.0 reduce-scatter.5.cloned.1.call-start
  95.1 1.7 fusion.25
  96.8 24.1 %all-gather.2.cloned.1.call-done = bf16[4,160,2,512]{3,1,0,2:T(8,128)(2,1)} async-done(((bf16[1,160,2,512]{3,1,0,2:T(8,128)(2,1)}), bf16[4,160,2,512]{3,1,0,2:T(8,128)(2,1)}) %all-gather.2.cloned.1.call-update) | async-done | bytes 1310736 | tf_op jit(solution)/shard_map/all_gather | solution.py:35
  120.9 137.7 %while.14 = (s32[]{:T(128)}, f32[640,2560]{1,0:T(8,128)}, bf16[640,2,512]{2,0,1:T(8,128)(2,1)}, bf16[160,2,512]{2,0,1:T(8,128)(2,1)S(1)}, s32[]{:T(128)}, /*index=5*/s32[]{:T(128)}) while((s32[]{:T(128)}, f32[640,2560]{1,0:T(8,128)}, bf16[640,2,512]{2,0,1:T(8,128)(2,1)}, bf16[160,2,512]{2,0,1:T(8,128)(2,1)S(1)}, s32[]{:T(128)}, ...), condition=%wide.region_2.3_spmd.clone, body=%wide.region_1.2_spmd.clone.sunk | while | flops 1680998400 | bytes 27361408 | solution.py:52
  120.9 1.7 stack.11
  122.7 8.4 %all-to-all-start = ((bf16[16,160,512]{2,1,0:T(8,128)(2,1)}), bf16[16,160,512]{2,1,0:T(8,128)(2,1)}, u32[]{:S(2)}, u32[]{:S(2)}) async-start(bf16[16,160,512]{2,1,0:T(8,128)(2,1)} %stack.11), calls=%async_computation | async-start | bytes 5242880 | tf_op jit(solution)/shard_map/while/body/eval_jaxpr/all_to_all | solution.py:46
  131.1 50.9 %all-to-all-done = bf16[16,160,512]{2,1,0:T(8,128)(2,1)} async-done(((bf16[16,160,512]{2,1,0:T(8,128)(2,1)}), bf16[16,160,512]{2,1,0:T(8,128)(2,1)}, u32[]{:S(2)}, u32[]{:S(2)}) %all-to-all-start) | async-done | bytes 2621472 | tf_op jit(solution)/shard_map/while/body/eval_jaxpr/all_to_all | solution.py:46
  182.0 6.6 %select_add_fusion.2 = f32[640,2560]{1,0:T(8,128)} fusion(f32[640,2560]{1,0:T(8,128)} %get-tuple-element.144, bf16[2560,512]{1,0:T(8,128)(2,1)} %bitcast.42, pred[]{:T(512)S(6)} %compare.17, bf16[640,2,512]{2,0,1:T(8,128)(2,1)} %get-tuple-element.151, s32[]{:T(128)S(6)} %copy.12), kind=kOutput, calls=%fused_computation.1.clone.1 | convolution fusion | flops 1680998400 | bytes 16384005 | tf_op jit(solution)/shard_map/while/body/eval_jaxpr/dot_general | solution.py:43
  188.6 1.7 stack.11
  190.3 13.0 %all-to-all-start = ((bf16[16,160,512]{2,1,0:T(8,128)(2,1)}), bf16[16,160,512]{2,1,0:T(8,128)(2,1)}, u32[]{:S(2)}, u32[]{:S(2)}) async-start(bf16[16,160,512]{2,1,0:T(8,128)(2,1)} %stack.11), calls=%async_computation | async-start | bytes 5242880 | tf_op jit(solution)/shard_map/while/body/eval_jaxpr/all_to_all | solution.py:46
  203.3 46.8 %all-to-all-done = bf16[16,160,512]{2,1,0:T(8,128)(2,1)} async-done(((bf16[16,160,512]{2,1,0:T(8,128)(2,1)}), bf16[16,160,512]{2,1,0:T(8,128)(2,1)}, u32[]{:S(2)}, u32[]{:S(2)}) %all-to-all-start) | async-done | bytes 2621472 | tf_op jit(solution)/shard_map/while/body/eval_jaxpr/all_to_all | solution.py:46
  250.1 8.5 %select_add_fusion.2 = f32[640,2560]{1,0:T(8,128)} fusion(f32[640,2560]{1,0:T(8,128)} %get-tuple-element.144, bf16[2560,512]{1,0:T(8,128)(2,1)} %bitcast.42, pred[]{:T(512)S(6)} %compare.17, bf16[640,2,512]{2,0,1:T(8,128)(2,1)} %get-tuple-element.151, s32[]{:T(128)S(6)} %copy.12), kind=kOutput, calls=%fused_computation.1.clone.1 | convolution fusion | flops 1680998400 | bytes 16384005 | tf_op jit(solution)/shard_map/while/body/eval_jaxpr/dot_general | solution.py:43
  258.6 5.0 %convert_element_type.18 = bf16[640,2560]{1,0:T(8,128)(2,1)} convert(f32[640,2560]{1,0:T(8,128)} %get-tuple-element.84) | non-fusion elementwise | flops 1638400 | bytes 9830400 | tf_op jit(solution)/shard_map/convert_element_type | solution.py:54
  263.6 0.0 reduce-scatter.5.cloned.1.call-update
  263.6 59.2 %reduce-scatter.5.cloned.1.call-done = bf16[160,2560]{1,0:T(8,128)(2,1)} async-done(((bf16[640,2560]{1,0:T(8,128)(2,1)}), bf16[160,2560]{1,0:T(8,128)(2,1)}) %reduce-scatter.5.cloned.1.call-update) | async-done | bytes 819216 | tf_op jit(solution)/shard_map/reduce_scatter | solution.py:53
  322.7 2.5 convert_element_type.19
  (5 shorter events, 0.0 us)
Async XLA Ops:
  6.5 22.7 %copy-start = (bf16[2560,512]{1,0:T(8,128)(2,1)S(1)}, bf16[2560,512]{1,0:T(8,128)(2,1)}, u32[]{:S(2)}) copy-start(bf16[2560,512]{1,0:T(8,128)(2,1)} %param.6) | copy-start | bytes 7864324
  6.5 86.1 %all-reduce.3.cloned.1.call-start = ((), (), s32[]{:S(2)}) async-start(), calls=%async_computation.4 | async-start | bytes 2621440
  29.3 9.4 %copy-start.1 = (u32[256]{0:T(256)S(1)}, u32[256]{0:T(256)}, u32[]{:S(2)}) copy-start(u32[256]{0:T(256)} %constant.82) | copy-start | bytes 3076
  38.7 82.3 %all-gather.2.cloned.1.call-start = ((), (), s32[]{:S(2)}) async-start(), calls=%async_computation.2 | async-start | bytes 1638400 | tf_op jit(solution)/shard_map/all_gather | solution.py:35
  95.0 227.7 %reduce-scatter.5.cloned.1.call-start = ((), (), s32[]{:S(2)}) async-start(), calls=%async_computation.3 | async-start | bytes 4096000 | tf_op jit(solution)/shard_map/reduce_scatter | solution.py:53
  122.7 59.3 %all-to-all-start = ((bf16[16,160,512]{2,1,0:T(8,128)(2,1)}), bf16[16,160,512]{2,1,0:T(8,128)(2,1)}, u32[]{:S(2)}, u32[]{:S(2)}) async-start(bf16[16,160,512]{2,1,0:T(8,128)(2,1)} %stack.11), calls=%async_computation | async-start | bytes 5242880 | tf_op jit(solution)/shard_map/while/body/eval_jaxpr/all_to_all | solution.py:46
  190.3 59.8 %all-to-all-start = ((bf16[16,160,512]{2,1,0:T(8,128)(2,1)}), bf16[16,160,512]{2,1,0:T(8,128)(2,1)}, u32[]{:S(2)}, u32[]{:S(2)}) async-start(bf16[16,160,512]{2,1,0:T(8,128)(2,1)} %stack.11), calls=%async_computation | async-start | bytes 5242880 | tf_op jit(solution)/shard_map/while/body/eval_jaxpr/all_to_all | solution.py:46
Sparse Core Ops, SparseCore 0:
  38.8 53.7 all-reduce.2
  95.1 25.7 all-gather.1
  263.7 59.0 reduce-scatter.4
